TPU v7x, 128 devices: a whole 4x4x4 slice. The times are simulated.
128 devices in a mesh: row: 8 (over y, x_lo), col: 16 (over x_hi, z, core).
Axes of the slice: x: 4 (x_hi: 2, x_lo: 2; x = x_hi * 2 + x_lo), y: 4, z: 4, core: 2. Of those that a mesh axis runs over, the one named last changes fastest.
Arguments:
- homolog_features: bfloat16 [128, 2048, 64], P('col', 'row'), may hold values from -6 to 6
- validity_indicator: int32 [128, 64], P('col', 'row'), may hold values from -2147483648 to 2147483647, as said below
- standardize_scaling: float32 [64], replicated, may hold values from 0.1 to 1.9
- source_projector: bfloat16 [64, 32], replicated, may hold values from -0.75 to 0.75
- target_projector: bfloat16 [64, 32], replicated, may hold values from -0.75 to 0.75
- final_projector: bfloat16 [1024, 128], replicated, may hold values from -0.75 to 0.75
- final_offset: float32 [128], replicated, may hold values from -3 to 3
Outputs:
- pair_update: bfloat16 [2048, 2048, 128], P('row', 'col')
Inputs may be any that keep to these rules, and one draw needn't show every extreme that they name: `validity_indicator`: bit k of word w of sequence s is the mask of residue 32 * w + k; some residues are masked in every sequence.
All inputs are finite; a program needn't handle non-finite values.
Results may differ from a plain program's by a relative error of at most 0.0069.
Values may be sent and summed in bfloat16 or wider, within the bound.
A program may use at most 128 MiB of HBM per device.

v0:
```python
import jax
import jax.numpy as jnp
from jax import lax
from jax.sharding import PartitionSpec as P


def unpack_mask(packed_words):
    positions = jnp.arange(32, dtype=jnp.int32)
    bit_values = jnp.bitwise_and(jnp.right_shift(packed_words[..., None], positions), 1)
    return bit_values.reshape(packed_words.shape[0], packed_words.shape[1] * 32)


def on_device(
    homolog_features,
    validity_indicator,
    standardize_scaling,
    source_projector,
    target_projector,
    final_projector,
    final_offset,
):
    tensor_products = homolog_features.astype(jnp.float32)
    center = jnp.mean(tensor_products, axis=-1, keepdims=True)
    spread = jnp.mean((tensor_products - center) ** 2, axis=-1, keepdims=True)
    normed = ((tensor_products - center) * lax.rsqrt(spread + 1e-05) * standardize_scaling).astype(
        jnp.bfloat16
    )
    weight_matrix = unpack_mask(validity_indicator).astype(jnp.float32)[..., None]
    source_embedding = (
        jnp.einsum("srm,mh->srh", normed, source_projector, preferred_element_type=jnp.float32)
        * weight_matrix
    ).astype(jnp.bfloat16)
    target_embedding = (
        jnp.einsum("srm,mh->srh", normed, target_projector, preferred_element_type=jnp.float32)
        * weight_matrix
    ).astype(jnp.bfloat16)
    left_all, rows_packed = (
        lax.all_gather(source_embedding, "col", axis=0, tiled=True),
        lax.all_gather(validity_indicator, "col", axis=0, tiled=True),
    )
    right_wide, wide_packed = (
        lax.all_gather(target_embedding, "row", axis=1, tiled=True),
        lax.all_gather(validity_indicator, "row", axis=1, tiled=True),
    )
    width = right_wide.shape[1] // lax.axis_size("col")
    right_full, full_packed = (
        lax.all_gather(right_wide, "col", axis=0, tiled=True),
        lax.all_gather(wide_packed, "col", axis=0, tiled=True),
    )
    begin = lax.axis_index("col") * width
    right_cols = lax.dynamic_slice_in_dim(right_full, begin, width, 1)
    cols_packed = lax.dynamic_slice_in_dim(full_packed, begin // 32, width // 32, 1)
    mask_rows = unpack_mask(rows_packed).astype(jnp.bfloat16)
    mask_cols = unpack_mask(cols_packed).astype(jnp.bfloat16)
    counts = jnp.dot(mask_rows.T, mask_cols, preferred_element_type=jnp.float32)
    denom = jnp.maximum(counts, 1.0)
    seq_total, row_count, channels = left_all.shape
    tiles_list = row_count // 16
    source_tiles = left_all.reshape(seq_total, tiles_list, 16, channels).transpose(1, 0, 2, 3)
    denom_blocks = denom.reshape(tiles_list, 16, width)
    pair_width = final_projector.shape[1]

    def one_block(args):
        piece, scale = args
        outer = jnp.einsum("sic,sje->ijce", piece, right_cols, preferred_element_type=jnp.float32)
        outer = outer.astype(jnp.bfloat16).reshape(16 * width, channels * channels)
        projected = jnp.dot(outer, final_projector, preferred_element_type=jnp.float32).reshape(
            16, width, pair_width
        )
        return (projected / scale[..., None] + final_offset).astype(jnp.bfloat16)

    result = lax.map(one_block, (source_tiles, denom_blocks))
    return result.reshape(row_count, width, pair_width)


def solution(mesh):
    in_specs = (P("col", "row", None), P("col", "row"), P(), P(), P(), P(), P())
    out_specs = P("row", "col", None)
    return jax.shard_map(
        on_device, mesh=mesh, in_specs=in_specs, out_specs=out_specs, check_vma=False
    )
```

profile of v0, /device:TPU:33, one launch (start us, length us, event | category | flops | bytes accessed | tf_op | source)
XLA Modules:
  0.0 307.7 jit_solution(3551284886635153795)
XLA Ops:
  9.6 1.9 fusion.10
  11.5 1.8 fusion.9
  13.4 35.9 %all-gather.6.cloned.1.call-done = bf16[8,2048,32]{1,2,0:T(8,128)(2,1)} async-done(((bf16[8,256,32]{1,2,0:T(8,128)(2,1)}), bf16[8,2048,32]{1,2,0:T(8,128)(2,1)}) %all-gather.6.cloned.1.call-update) | async-done | bytes 1048592 | tf_op jit(solution)/shard_map/all_gather | solution.py:42
  50.2 22.1 %all_gather.22 = s32[8,64]{0,1:T(8,128)S(1)} all-gather(s32[8,8]{0,1:T(8,128)S(1)} %copy.26), channel_id=1, replica_groups=mesh['row'=8,'col'=16] {'row'}, dimensions={1}, use_global_device_ids=true | all-gather | bytes 2304 | tf_op jit(solution)/shard_map/all_gather | solution.py:43
  72.3 30.9 %all_gather.23 = s32[128,64]{1,0:T(8,128)S(1)} all-gather(s32[8,64]{1,0:T(8,128)S(1)} %copy.27), channel_id=1, replica_groups=mesh['row'=8,'col'=16] {'col'}, dimensions={0}, use_global_device_ids=true | all-gather | bytes 34816 | tf_op jit(solution)/shard_map/all_gather | solution.py:48
  103.4 24.3 %all_gather.21 = s32[128,8]{1,0:T(8,128)S(1)} all-gather(s32[8,8]{1,0:T(8,128)} %param.10), channel_id=1, replica_groups=mesh['row'=8,'col'=16] {'col'}, dimensions={0}, use_global_device_ids=true | all-gather | bytes 4352 | tf_op jit(solution)/shard_map/all_gather | solution.py:39
  128.0 4.3 %copy.24 = bf16[128,256,32]{0,2,1:T(8,128)(2,1)S(1)} copy(bf16[128,256,32]{1,2,0:T(8,128)(2,1)} %all-gather.4.cloned.1.call-done) | data formatting | bytes 4194304 | tf_op jit(solution)/shard_map/all_gather | solution.py:38
  132.3 82.3 %all-gather.8.cloned.1.call-done = bf16[128,2048,32]{1,2,0:T(8,128)(2,1)} async-done(((bf16[8,2048,32]{1,2,0:T(8,128)(2,1)}), bf16[128,2048,32]{1,2,0:T(8,128)(2,1)}) %all-gather.8.cloned.1.call-update) | async-done | bytes 16777232 | tf_op jit(solution)/shard_map/all_gather | solution.py:47
  216.4 84.8 %while.10 = (s32[]{:T(128)}, bf16[16,16,128,128]{3,2,1,0:T(8,128)(2,1)}, bf16[16,128,16,32]{1,3,2,0:T(8,128)(2,1)S(1)}, bf16[128,128,32]{1,0,2:T(8,128)(2,1)S(1)...) while((s32[]{:T(128)}, ...), condition=%wide.region_3.4_spmd, body=%wide.region_2.3_spmd.sunk | while | flops 1076625408 | bytes 18768988 | solution.py:72
  219.4 2.3 fusion.32
  222.9 1.8 copy.33
  224.7 2.3 fusion.32
  230.0 2.3 fusion.32
  233.5 1.8 copy.33
  235.3 2.3 fusion.32
  238.8 1.8 copy.33
  240.6 2.3 fusion.32
  245.9 2.3 fusion.32
  249.4 1.8 copy.33
  251.2 2.3 fusion.32
  256.5 2.3 fusion.32
  261.8 2.3 fusion.32
  267.1 2.3 fusion.32
  272.4 2.3 fusion.32
  275.9 1.8 copy.33
  277.7 2.3 fusion.32
  283.0 2.3 fusion.32
  286.5 1.8 copy.33
  288.3 2.3 fusion.32
  291.8 1.8 copy.33
  293.6 2.3 fusion.32
  298.9 2.3 fusion.32
  (74 shorter events, 42.0 us)
Async XLA Ops:
  6.5 3.1 copy-start
  6.5 209.8 %copy-start.1 = (bf16[1024,128]{1,0:T(8,128)(2,1)S(1)}, bf16[1024,128]{1,0:T(8,128)(2,1)}, u32[]{:S(2)}) copy-start(bf16[1024,128]{1,0:T(8,128)(2,1)} %param.14) | copy-start | bytes 786436
  6.5 209.8 %copy-start.2 = (f32[128]{0:T(128)S(1)}, f32[128]{0:T(128)}, u32[]{:S(2)}) copy-start(f32[128]{0:T(128)} %param.15) | copy-start | bytes 1540
  6.5 42.8 %all-gather.6.cloned.1.call-start = ((), (), s32[]{:S(2)}) async-start(), calls=%async_computation.1 | async-start | bytes 1179648 | tf_op jit(solution)/shard_map/all_gather | solution.py:42
  11.5 116.5 %all-gather.4.cloned.1.call-start = ((), (), s32[]{:S(2)}) async-start(), calls=%async_computation | async-start | bytes 2228224 | tf_op jit(solution)/shard_map/all_gather | solution.py:38
  13.4 201.3 %all-gather.8.cloned.1.call-start = ((), (), s32[]{:S(2)}) async-start(), calls=%async_computation.2 | async-start | bytes 17825792 | tf_op jit(solution)/shard_map/all_gather | solution.py:47
Sparse Core Ops, SparseCore 0:
  11.6 37.7 all-gather.5
  51.8 53.3 all-gather.3
  107.7 106.9 all-gather.7
where the time goes:
time: 311 us; the launch traced here: 308 us
  waiting for transfers between devices  118 us (38%)
  blocking collectives  77.3 us (25%)
  matrix products  59.9 us (19%)
  local copies, waits for them, and re-layouts  36.4 us (12%)
  between operations  13.2 us (4%)
    all_gather x1, waiting for transfers between devices, on_device(): lax.all_gather(right_wide, 'col', axis=0, tiled=True)  82.3 us
    dot_general x16, matrix products, one_block(): jnp.dot(outer, final_projector, preferred_element_type=jnp.float32)  36.2 us
    all_gather x1, waiting for transfers between devices, on_device(): lax.all_gather(target_embedding, 'row', axis=1, tiled=True)  35.9 us
    all_gather x1, blocking collectives, on_device(): lax.all_gather(wide_packed, 'col', axis=0, tiled=True)  30.9 us
    convert_element_type x16, local copies, waits for them, and re-layouts, one_block(): outer = outer.astype(jnp.bfloat16).reshape(16 * width, channels * channels)  28.2 us
    all_gather x1, blocking collectives, on_device(): lax.all_gather(validity_indicator, 'col', axis=0, tiled=True)  24.3 us
    all_gather x1, blocking collectives, on_device(): lax.all_gather(validity_indicator, 'row', axis=1, tiled=True)  22.1 us
    dot_general x16, matrix products, one_block(): jnp.einsum('sic,sje->ijce', piece, right_cols, preferred_element_type=jnp...  19.8 us
  transfers between devices with their start and end apart: 3, of which 2 were waited for; matrix products, arithmetic and copies ran while one was open for 2% of the time, Pallas kernels for 0%

commit v1 on v0

v1 whole, which is shorter than its diff:
```python
import functools

import jax
import jax.numpy as jnp
from jax import lax
from jax.experimental import pallas as pl
from jax.experimental.pallas import tpu as pltpu
from jax.sharding import PartitionSpec as P

BF16 = jnp.bfloat16
F32 = jnp.float32
MESH = pl.DeviceIdType.MESH

SEQS = 8
ROWS = 256
COLS = 128
WIDTH = 32
DEPTH = 64
CZ = 128
SLOTS = 16
PARTS = 4
L_ROWS = 16 + ROWS // 4 * SEQS
R_ROWS = 16 + WIDTH * SEQS
L_STEP = (L_ROWS - 16) // PARTS
R_STEP = (R_ROWS - 16) // PARTS


def span(step, part):
    return pl.ds(0, 16 + step) if part == 0 else pl.ds(16 + step * part, step)


class Place:
    def __init__(self):
        self.row = lax.axis_index("row")
        self.col = lax.axis_index("col")
        self.y, self.xl = self.row // 2, self.row % 2
        chip = self.col // 2
        self.xh, self.z, self.core = chip // 4, chip % 4, self.col % 2
        self.slot = self.z * 4 + self.xh * 2 + self.core
        self.to_xh, self.to_z = self.y // 2, self.row % 4
        self.relay_y = (self.y + self.z - self.to_z + 4) % 4
        self.from_y, self.from_xl = self.xh * 2 + self.z // 2, self.z % 2

    def near_z(self, y):
        return (y - self.from_y + self.z + 8) % 4

    def device(self, y=None, xl=None, xh=None, z=None, core=None):
        pick = lambda a, b: b if a is None else a
        y, xl, xh = pick(y, self.y), pick(xl, self.xl), pick(xh, self.xh)
        z, core = pick(z, self.z), pick(core, self.core)
        return (y * 2 + xl, (xh * 4 + z) * 2 + core)

    def is_me(self, device):
        return (device[0] == self.row) & (device[1] == self.col)


def normalise(xv, gain_ref, ns, nt):
    gain = jnp.broadcast_to(gain_ref[...], (ROWS, DEPTH)).T
    for s in range(SEQS):
        x = xv[s].astype(F32)
        center = jnp.mean(x, axis=0, keepdims=True)
        d = x - center
        spread = jnp.mean(d * d, axis=0, keepdims=True)
        normed = d * lax.rsqrt(spread + 1e-05) * gain
        nt[s] = normed.astype(BF16)
        ns[pl.ds(s * ROWS, ROWS), :] = normed.T


def masks_by_half(v):
    lane = lax.broadcasted_iota(jnp.int32, (SEQS, 128), 1)
    out = []
    for h in range(2):
        word = jnp.broadcast_to(v[:, 4 * h : 4 * h + 1], (SEQS, 128))
        for q in range(1, 4):
            word = jnp.where(lane // 32 == q, v[:, 4 * h + q : 4 * h + q + 1], word)
        out.append((lax.shift_right_logical(word, lane % 32) & 1).astype(F32))
    return out


def project_right(nt, pt_ref, masks, rs, rsend):
    for s in range(SEQS):
        y = jnp.dot(pt_ref[...], nt[s], preferred_element_type=F32)
        for h in range(2):
            rs[h, pl.ds(s, WIDTH, stride=SEQS), :] = y[:, h * COLS : (h + 1) * COLS]
    tile = jnp.concatenate(masks, axis=0).astype(BF16)
    for h in range(2):
        rsend[h, 0:16, :] = tile
        block = rs[h].reshape(WIDTH, SEQS, COLS) * masks[h][None]
        rsend[h, 16:R_ROWS, :] = block.reshape(WIDTH * SEQS, COLS).astype(BF16)


def project_left(ns, ps_ref, v, masks, lbuf, slot):
    total = None
    p = ps_ref[...].astype(F32).T.astype(BF16)
    zero = jnp.zeros_like(p)
    for a in range(4):
        n = jnp.concatenate(
            [ns[pl.ds(4 * b + a, SEQS, stride=ROWS), :] for b in range(ROWS // 4)], axis=0
        ).astype(BF16)
        wide = jnp.concatenate([p if q == a else zero for q in range(4)], axis=1)
        part = jnp.dot(n, wide, preferred_element_type=F32)
        total = part if total is None else total + part
    shift = lax.broadcasted_iota(jnp.int32, (SEQS, 128), 1) // 32
    mask = []
    for b in range(ROWS // 4):
        word = jnp.broadcast_to(v[:, b // 8 : b // 8 + 1], (SEQS, 128))
        mask.append((lax.shift_right_logical(word, shift + (b % 8) * 4) & 1).astype(F32))
    out = total * jnp.concatenate(mask, axis=0)
    lbuf[slot, 0:16, :] = jnp.concatenate(masks, axis=0).astype(BF16)
    lbuf[slot, 16:L_ROWS, :] = out.astype(BF16)


def reorder_final(wv, wf, wt):
    wf[...] = wv[...].astype(F32)
    for part in range(8):
        rows = [wf[pl.ds(4 * part + e, WIDTH, stride=WIDTH), :] for e in range(4)]
        wt[:, part * 128 : (part + 1) * 128] = jnp.concatenate(rows, axis=0).astype(BF16).T


def unpack_left(lbuf, a_ref, part):
    block = lbuf[:, 16 + L_STEP * part : 16 + L_STEP * (part + 1), :].astype(F32)
    groups = L_STEP // SEQS
    block = block.reshape(SLOTS, groups, SEQS, 128)
    for b in range(groups):
        tile = block[:, b].reshape(SLOTS * SEQS, 128).astype(BF16)
        a_ref[pl.ds((part * groups + b) * 128, 128), :] = tile.T


def unpack_right(rbuf, r_ref, part):
    block = rbuf[:, 16 + R_STEP * part : 16 + R_STEP * (part + 1), :].astype(F32)
    groups = R_STEP // SEQS
    block = block.reshape(SLOTS, groups, SEQS, COLS)
    for e in range(groups):
        at = (part * groups + e) * COLS
        r_ref[:, at : at + COLS] = block[:, e].reshape(SLOTS * SEQS, COLS).astype(BF16)


def count_pairs(lbuf, rbuf, core, rc_ref):
    mi = lbuf[:, 0:16, :].astype(F32).reshape(SLOTS, 2, SEQS, 128)
    mj = rbuf[:, 0:16, :].astype(F32).reshape(SLOTS, 2, SEQS, 128)
    first = (core == 0).astype(F32)
    cols = (mj[:, 0] * first + mj[:, 1] * (1.0 - first)).reshape(128, 128).astype(BF16)
    for h in range(2):
        rows = mi[:, h].reshape(128, 128).astype(BF16)
        counts = lax.dot_general(rows, cols, (((0,), (0,)), ((), ())), preferred_element_type=F32)
        rc_ref[pl.ds(h * 128, 128), :] = 1.0 / jnp.maximum(counts, 1.0)


def gather_kernel(
    x_hbm, v_ref, gain_ref, ps_ref, pt_ref, w_hbm, off_ref,
    a_ref, r_ref, wt_ref, rc_ref, ob_ref,
    xv, wv, wf, ns, nt, rs, rsend, lbuf, rbuf,
    in_sem, rs1, rr1, rs2, rr2, ls, lr, fs, fr,
):
    me = Place()
    x_copy = pltpu.make_async_copy(x_hbm, xv, in_sem.at[0])
    w_copy = pltpu.make_async_copy(w_hbm, wv, in_sem.at[1])
    x_copy.start()
    w_copy.start()

    shifts = [(a, b) for a in range(2) for b in range(4) if (a, b) != (0, 0)]
    partner = me.device(core=1 - me.core)
    aways = [me.device(xh=(me.xh + a) % 2, z=(me.z + b) % 4) for a, b in shifts]
    froms = [((me.xh + a) % 2, (me.z + 4 - b) % 4) for a, b in shifts]
    relays = [
        (h, me.device(y=me.relay_y, xl=xl, xh=me.to_xh, z=me.to_z, core=h))
        for h in range(2) for xl in range(2)
    ]
    near = me.near_z(me.y)
    sources = [
        me.device(y=me.from_y, xl=me.from_xl, xh=xh, z=near, core=c)
        for xh in range(2) for c in range(2)
    ]
    others = [me.device(y=(me.y + d) % 4) for d in (1, 2, 3)]
    bar = pltpu.get_barrier_semaphore()
    friends = aways + [partner] + [d for _, d in relays] + sources + others
    for device in friends:
        pl.semaphore_signal(bar, inc=1, device_id=device, device_id_type=MESH)

    x_copy.wait()
    v = v_ref[...]
    masks = masks_by_half(v)
    normalise(xv, gain_ref, ns, nt)
    project_right(nt, pt_ref, masks, rs, rsend)
    project_left(ns, ps_ref, v, masks, lbuf, me.slot)

    pl.semaphore_wait(bar, len(friends))

    def first_copy(part, n):
        h, device = relays[n]
        rows = span(R_STEP, part)
        return pltpu.make_async_remote_copy(
            src_ref=rsend.at[h, rows], dst_ref=rbuf.at[me.slot, rows],
            send_sem=rs1.at[part, n], recv_sem=rr1.at[part, me.xh * 2 + me.core],
            device_id=device, device_id_type=MESH,
        )

    def second_copy(part, n):
        block = rbuf.at[pl.ds(near * 4, 4), span(R_STEP, part)]
        return pltpu.make_async_remote_copy(
            src_ref=block, dst_ref=block, send_sem=rs2.at[part, n], recv_sem=rr2.at[part, n],
            device_id=others[n], device_id_type=MESH,
        )

    def left_copy(part, n):
        piece = lbuf.at[me.slot, span(L_STEP, part)]
        return pltpu.make_async_remote_copy(
            src_ref=piece, dst_ref=piece, send_sem=ls.at[part, n], recv_sem=lr.at[part, n],
            device_id=(aways + [partner])[n], device_id_type=MESH,
        )

    def pass_on_copy(part, n):
        xh, z = froms[n]
        piece = lbuf.at[z * 4 + xh * 2 + me.core, span(L_STEP, part)]
        return pltpu.make_async_remote_copy(
            src_ref=piece, dst_ref=piece, send_sem=fs.at[part, n], recv_sem=fr.at[part, n],
            device_id=partner, device_id_type=MESH,
        )

    def start_first(part):
        rows = span(R_STEP, part)
        for n, (h, device) in enumerate(relays):
            mine = me.is_me(device)

            @pl.when(jnp.logical_not(mine))
            def _():
                first_copy(part, n).start()

            @pl.when(mine)
            def _():
                rbuf[me.slot, rows, :] = rsend[h, rows, :]

    def relay(part):
        rows = span(R_STEP, part)
        for n, device in enumerate(sources):
            @pl.when(jnp.logical_not(me.is_me(device)))
            def _():
                pltpu.make_async_remote_copy(
                    src_ref=rsend.at[0, rows], dst_ref=rbuf.at[near * 4 + n, rows],
                    send_sem=rs1.at[part, 0], recv_sem=rr1.at[part, n],
                    device_id=device, device_id_type=MESH,
                ).wait_recv()
        for n in range(3):
            second_copy(part, n).start()

    def pass_on(part):
        for n in range(7):
            left_copy(part, n).wait_recv()
            pass_on_copy(part, n).start()

    for part in range(PARTS):
        start_first(part)
        for n in range(8):
            left_copy(part, n).start()

    w_copy.wait()
    reorder_final(wv, wf, wt_ref)
    ob_ref[...] = jnp.broadcast_to(off_ref[...], (CZ, CZ)).T

    for part in range(PARTS):
        relay(part)
        pass_on(part)

    for part in range(PARTS):
        for n in range(3):
            second_copy(part, n).wait_recv()
        left_copy(part, 7).wait_recv()
        for n in range(7):
            pass_on_copy(part, n).wait_recv()
        if part == 0:
            count_pairs(lbuf, rbuf, me.core, rc_ref)
        unpack_right(rbuf, r_ref, part)
        unpack_left(lbuf, a_ref, part)

    for part in range(PARTS):
        for n, (_, device) in enumerate(relays):
            @pl.when(jnp.logical_not(me.is_me(device)))
            def _():
                first_copy(part, n).wait_send()
        for n in range(3):
            second_copy(part, n).wait_send()
        for n in range(8):
            left_copy(part, n).wait_send()
        for n in range(7):
            pass_on_copy(part, n).wait_send()


def gather(x, v, gain, ps, pt, w, off):
    vmem = pl.BlockSpec(memory_space=pltpu.VMEM)
    hbm = pl.BlockSpec(memory_space=pl.ANY)
    dma = pltpu.SemaphoreType.DMA
    return pl.pallas_call(
        gather_kernel,
        out_shape=[
            jax.ShapeDtypeStruct((ROWS * WIDTH, 128), BF16),
            jax.ShapeDtypeStruct((128, WIDTH * COLS), BF16),
            jax.ShapeDtypeStruct((CZ, WIDTH * WIDTH), BF16),
            jax.ShapeDtypeStruct((ROWS, COLS), F32),
            jax.ShapeDtypeStruct((CZ, CZ), F32),
        ],
        in_specs=[hbm, vmem, vmem, vmem, vmem, hbm, vmem],
        out_specs=[vmem] * 5,
        scratch_shapes=[
            pltpu.VMEM((SEQS, DEPTH, ROWS), BF16),
            pltpu.VMEM((WIDTH * WIDTH, CZ), BF16),
            pltpu.VMEM((WIDTH * WIDTH, CZ), F32),
            pltpu.VMEM((SEQS * ROWS, DEPTH), F32),
            pltpu.VMEM((SEQS, DEPTH, ROWS), BF16),
            pltpu.VMEM((2, WIDTH * SEQS, COLS), F32),
            pltpu.VMEM((2, R_ROWS, COLS), BF16),
            pltpu.VMEM((SLOTS, L_ROWS, 128), BF16),
            pltpu.VMEM((SLOTS, R_ROWS, COLS), BF16),
            dma((2,)),
            dma((PARTS, 4)), dma((PARTS, 4)), dma((PARTS, 3)), dma((PARTS, 3)),
            dma((PARTS, 8)), dma((PARTS, 8)), dma((PARTS, 7)), dma((PARTS, 7)),
        ],
        compiler_params=pltpu.CompilerParams(
            collective_id=0, has_side_effects=True, vmem_limit_bytes=48 * 2**20
        ),
        name="gather_factors",
    )(x, v, gain, ps, pt, w, off)


def pair_kernel(a_ref, r_ref, wt_ref, rc_ref, ob_ref, out_ref, outer, *, block):
    a = a_ref[...]
    for p in range(WIDTH // 2):
        x = jnp.dot(a, r_ref[:, p * 256 : (p + 1) * 256], preferred_element_type=F32).astype(BF16)
        for i in range(block):
            for e in range(2):
                outer[i // 2, (2 * p + e) * 32 : (2 * p + e + 1) * 32, (i % 2) * 128 : (i % 2 + 1) * 128] = x[
                    i * 32 : (i + 1) * 32, e * 128 : (e + 1) * 128
                ]
    for k in range(block // 2):
        y = jnp.dot(wt_ref[...], outer[k], preferred_element_type=F32)
        for h in range(2):
            i = 2 * k + h
            value = y[:, h * 128 : (h + 1) * 128] * rc_ref[i : i + 1, :] + ob_ref[...]
            out_ref[i] = value.astype(BF16).T


def pairs(a, r, wt, rc, ob, block=32):
    return pl.pallas_call(
        functools.partial(pair_kernel, block=block),
        grid=(ROWS // block,),
        in_specs=[
            pl.BlockSpec((block * WIDTH, 128), lambda t: (t, 0)),
            pl.BlockSpec((128, WIDTH * COLS), lambda t: (0, 0)),
            pl.BlockSpec((CZ, WIDTH * WIDTH), lambda t: (0, 0)),
            pl.BlockSpec((block, COLS), lambda t: (t, 0)),
            pl.BlockSpec((CZ, CZ), lambda t: (0, 0)),
        ],
        out_specs=pl.BlockSpec((block, COLS, CZ), lambda t: (t, 0, 0)),
        out_shape=jax.ShapeDtypeStruct((ROWS, COLS, CZ), BF16),
        scratch_shapes=[pltpu.VMEM((block // 2, WIDTH * WIDTH, 256), BF16)],
        compiler_params=pltpu.CompilerParams(vmem_limit_bytes=56 * 2**20),
        name="pair_update",
    )(a, r, wt, rc, ob)


def on_device(x, v, gain, ps, pt, w, off):
    a, r, wt, rc, ob = gather(
        x.transpose(0, 2, 1), v, gain.reshape(1, DEPTH), ps.T, pt.T, w, off.reshape(1, CZ)
    )
    return pairs(a, r, wt, rc, ob)


def solution(mesh):
    in_specs = (P("col", "row", None), P("col", "row"), P(), P(), P(), P(), P())
    return jax.shard_map(
        on_device, mesh=mesh, in_specs=in_specs, out_specs=P("row", "col", None), check_vma=False
    )
```

time: 311 us -> 84.1 us (0.27)
  waiting for transfers between devices: 118 us -> 0 us
  blocking collectives: 77.3 us -> 0 us
  Pallas kernels: 0 us -> 74.2 us
  matrix products: 59.9 us -> 0 us
  local copies, waits for them, and re-layouts: 36.4 us -> 9.56 us
  between operations: 13.2 us -> 0.03 us
    all_gather x3 -> x0, waiting for transfers between devices: 118 us -> none  [the longest x1 82.3 us: on_device(): lax.all_gather(right_wide, 'col', axis=0, tiled=True)]
    all_gather x3 -> x0, blocking collectives: 77.3 us -> none  [the longest x1 30.9 us: on_device(): lax.all_gather(wide_packed, 'col', axis=0, tiled=True)]
    pallas_call x0 -> x2, Pallas kernels: none -> 74.2 us  [the longest x1 43.6 us: gather(): pl.pallas_call(gather_kernel, out_shape=[jax.ShapeDtypeStruct((ROWS * WID...]
    dot_general x35 -> x0, matrix products: 59.9 us -> none  [the longest x16 36.2 us: one_block(): jnp.dot(outer, final_projector, preferred_element_type=jnp.float32)]
    convert_element_type x16 -> x0, local copies, waits for them, and re-layouts: 28.2 us -> none  [one_block(): outer = outer.astype(jnp.bfloat16).reshape(16 * width, channels * channels)]
    unnamed x7 -> x24, local copies, waits for them, and re-layouts: 0.77 us -> 9.56 us
    all_gather x3 -> x0, local copies, waits for them, and re-layouts: 4.44 us -> none  [the longest x1 4.33 us: on_device(): lax.all_gather(source_embedding, 'col', axis=0, tiled=True)]
  transfers between devices with their start and end apart: 3 -> 0, of which waited for: 2 -> 0; matrix products, arithmetic and copies ran while one was open for 2% -> 0% of each run, Pallas kernels for 0% -> 0%
where the time goes in v1:
time: 84.1 us; the launch traced here: 83.8 us
  Pallas kernels  74.2 us (88%)
  local copies, waits for them, and re-layouts  9.56 us (11%)
    pallas_call x1, Pallas kernels, gather(): pl.pallas_call(gather_kernel, out_shape=[jax.ShapeDtypeStruct((ROWS * WID...  43.6 us
    pallas_call x1, Pallas kernels, pairs(): pl.pallas_call(functools.partial(pair_kernel, block=block), grid=(ROWS //...  30.6 us
    unnamed x24, local copies, waits for them, and re-layouts  9.56 us

profile of v1, /device:TPU:33, one launch (start us, length us, event | category | flops | bytes accessed | tf_op | source)
XLA Modules:
  0.0 83.8 jit_solution(4662236142154088253)
XLA Ops:
  0.0 0.0 copy-start.3
  0.0 0.9 %copy-done.3 = bf16[8,256,64]{1,2,0:T(8,128)(2,1)S(1)} copy-done((bf16[8,256,64]{1,2,0:T(8,128)(2,1)S(1)}, bf16[8,256,64]{1,2,0:T(8,128)(2,1)}, u32[]{:S(2)}) %copy-start.3) | copy-done | bytes 262168
  1.0 0.0 copy-start.4
  1.0 0.9 %copy-done.4 = bf16[1024,128]{1,0:T(8,128)(2,1)S(1)} copy-done((bf16[1024,128]{1,0:T(8,128)(2,1)S(1)}, bf16[1024,128]{1,0:T(8,128)(2,1)}, u32[]{:S(2)}) %copy-start.4) | copy-done | bytes 262168
  1.9 0.0 copy-start.7
  1.9 0.7 copy-done.7
  2.6 0.0 copy-start.8
  2.6 0.7 copy-done.8
  3.3 0.0 copy-start.9
  3.3 0.7 copy-done.9
  4.0 0.0 copy-start.10
  4.0 0.7 copy-done.10
  4.6 0.0 copy-start.11
  4.6 0.7 copy-done.11
  5.3 43.6 %gather_factors.1 = (bf16[8192,128]{1,0:T(8,128)(2,1)S(1)}, bf16[128,4096]{1,0:T(8,128)(2,1)S(1)}, bf16[128,1024]{1,0:T(8,128)(2,1)S(1)}, f32[256,128]{1,0:T(8,128)S(1)}, f32[128,128]{1,0:T(8,128)S(1)}) custom-call(bf16[8,64,256]{2,1,0:T(8,128)(2,1)S(1)} %bitcast.5, s32[8,8]{1,0:T(8,128)S(1)} %copy-done.9, f32[1,64]{1,0:T(1,128)S(1)} %bitcast.8, ...), custom_call_target="tpu_custom_call" | custom-call | tf_op jit(solution)/shard_map/gather_factors/pallas_call | solution.py:292
  48.9 0.0 copy-start
  49.0 1.3 %copy-done = bf16[8192,128]{1,0:T(8,128)(2,1)} copy-done((bf16[8192,128]{1,0:T(8,128)(2,1)}, bf16[8192,128]{1,0:T(8,128)(2,1)S(1)}, u32[]{:S(2)}) %copy-start) | copy-done | bytes 2097176
  50.3 0.0 copy-start.1
  50.3 1.0 %copy-done.1 = bf16[128,4096]{1,0:T(8,128)(2,1)} copy-done((bf16[128,4096]{1,0:T(8,128)(2,1)}, bf16[128,4096]{1,0:T(8,128)(2,1)S(1)}, u32[]{:S(2)}) %copy-start.1) | copy-done | bytes 1048600
  51.3 0.0 copy-start.2
  51.3 0.7 copy-done.2
  52.0 0.0 copy-start.5
  52.0 0.6 copy-done.5
  52.6 0.0 copy-start.6
  52.6 0.6 copy-done.6
  53.2 30.6 %pair_update.1 = bf16[256,128,128]{2,1,0:T(8,128)(2,1)} custom-call(bf16[8192,128]{1,0:T(8,128)(2,1)} %copy-done, bf16[128,4096]{1,0:T(8,128)(2,1)} %copy-done.1, bf16[128,1024]{1,0:T(8,128)(2,1)} %copy-done.2, f32[256,128]{1,0:T(8,128)} %copy-done.5, f32[128,128]{1,0:T(8,128)} %copy-done.6), custom_call_target="tpu_custom_call" | custom-call | tf_op jit(solution)/shard_map/pair_update/pallas_call | solution.py:342
Async XLA Ops:
  0.0 0.9 %copy-start.3 = (bf16[8,256,64]{1,2,0:T(8,128)(2,1)S(1)}, bf16[8,256,64]{1,2,0:T(8,128)(2,1)}, u32[]{:S(2)}) copy-start(bf16[8,256,64]{1,2,0:T(8,128)(2,1)} %param.7) | copy-start | bytes 786436
  1.0 0.9 %copy-start.4 = (bf16[1024,128]{1,0:T(8,128)(2,1)S(1)}, bf16[1024,128]{1,0:T(8,128)(2,1)}, u32[]{:S(2)}) copy-start(bf16[1024,128]{1,0:T(8,128)(2,1)} %w_hbm.1) | copy-start | bytes 786436
  1.9 0.7 copy-start.7
  2.6 0.7 copy-start.8
  3.3 0.7 copy-start.9
  4.0 0.7 copy-start.10
  4.6 0.7 copy-start.11
  48.9 1.3 %copy-start = (bf16[8192,128]{1,0:T(8,128)(2,1)}, bf16[8192,128]{1,0:T(8,128)(2,1)S(1)}, u32[]{:S(2)}) copy-start(bf16[8192,128]{1,0:T(8,128)(2,1)S(1)} %get-tuple-element.10.a_ref) | copy-start | bytes 6291460
  50.3 1.0 %copy-start.1 = (bf16[128,4096]{1,0:T(8,128)(2,1)}, bf16[128,4096]{1,0:T(8,128)(2,1)S(1)}, u32[]{:S(2)}) copy-start(bf16[128,4096]{1,0:T(8,128)(2,1)S(1)} %get-tuple-element.11.r_ref) | copy-start | bytes 3145732
  51.3 0.7 copy-start.2
  52.0 0.6 copy-start.5
  52.6 0.6 copy-start.6

commit v2 on v1

v2 whole, which is shorter than its diff:
```python
import jax
import jax.numpy as jnp
from jax import lax
from jax.experimental import pallas as pl
from jax.experimental.pallas import tpu as pltpu
from jax.sharding import PartitionSpec as P

BF16 = jnp.bfloat16
F32 = jnp.float32
MESH = pl.DeviceIdType.MESH

SEQS = 8
ROWS = 256
COLS = 128
WIDTH = 32
DEPTH = 64
CZ = 128
SLOTS = 16
PARTS = 4
L_ROWS = 16 + ROWS // 4 * SEQS
R_ROWS = 16 + WIDTH * SEQS
HALF = ROWS // 2
STEP = 64
BLOCK = 32
L_STEP = (L_ROWS - 16) // PARTS
R_STEP = (R_ROWS - 16) // PARTS


def span(step, part):
    return pl.ds(0, 16 + step) if part == 0 else pl.ds(16 + step * part, step)


class Place:
    def __init__(self):
        self.row = lax.axis_index("row")
        self.col = lax.axis_index("col")
        self.y, self.xl = self.row // 2, self.row % 2
        chip = self.col // 2
        self.xh, self.z, self.core = chip // 4, chip % 4, self.col % 2
        self.slot = self.z * 4 + self.xh * 2 + self.core
        self.to_xh, self.to_z = self.y // 2, self.row % 4
        self.relay_y = (self.y + self.z - self.to_z + 4) % 4
        self.relay_xl = (self.xl + self.xh + self.to_xh) % 2
        self.from_y, self.from_xl = self.xh * 2 + self.z // 2, self.z % 2

        self.near_z = (self.y - self.from_y + self.z + 4) % 4
        self.near_xh = (self.xl + self.from_xl + self.xh) % 2

    def device(self, y=None, xl=None, xh=None, z=None, core=None):
        pick = lambda a, b: b if a is None else a
        y, xl, xh = pick(y, self.y), pick(xl, self.xl), pick(xh, self.xh)
        z, core = pick(z, self.z), pick(core, self.core)
        return (y * 2 + xl, (xh * 4 + z) * 2 + core)

    def is_me(self, device):
        return (device[0] == self.row) & (device[1] == self.col)


def normalise(xv, gain_ref, ns, nt):
    gain = jnp.broadcast_to(gain_ref[...], (ROWS, DEPTH)).T
    for s in range(SEQS):
        x = xv[s].astype(F32)
        center = jnp.mean(x, axis=0, keepdims=True)
        d = x - center
        spread = jnp.mean(d * d, axis=0, keepdims=True)
        normed = d * lax.rsqrt(spread + 1e-05) * gain
        nt[s] = normed.astype(BF16)
        ns[pl.ds(s * ROWS, ROWS), :] = normed.T


def masks_by_half(v):
    lane = lax.broadcasted_iota(jnp.int32, (SEQS, 128), 1)
    out = []
    for h in range(2):
        word = jnp.broadcast_to(v[:, 4 * h : 4 * h + 1], (SEQS, 128))
        for q in range(1, 4):
            word = jnp.where(lane // 32 == q, v[:, 4 * h + q : 4 * h + q + 1], word)
        out.append((lax.shift_right_logical(word, lane % 32) & 1).astype(F32))
    return out


def project_right(nt, pt_ref, masks, rs, rsend):
    for s in range(SEQS):
        y = jnp.dot(pt_ref[...], nt[s], preferred_element_type=F32)
        for h in range(2):
            rs[h, pl.ds(s, WIDTH, stride=SEQS), :] = y[:, h * COLS : (h + 1) * COLS]
    tile = jnp.concatenate(masks, axis=0).astype(BF16)
    for h in range(2):
        rsend[h, 0:16, :] = tile
        block = rs[h].reshape(WIDTH, SEQS, COLS) * masks[h][None]
        rsend[h, 16:R_ROWS, :] = block.reshape(WIDTH * SEQS, COLS).astype(BF16)


def project_left(ns, ps_ref, v, masks, lbuf, slot):
    total = None
    p = ps_ref[...].astype(F32).T.astype(BF16)
    zero = jnp.zeros_like(p)
    for a in range(4):
        n = jnp.concatenate(
            [ns[pl.ds(4 * b + a, SEQS, stride=ROWS), :] for b in range(ROWS // 4)], axis=0
        ).astype(BF16)
        wide = jnp.concatenate([p if q == a else zero for q in range(4)], axis=1)
        part = jnp.dot(n, wide, preferred_element_type=F32)
        total = part if total is None else total + part
    shift = lax.broadcasted_iota(jnp.int32, (SEQS, 128), 1) // 32
    mask = []
    for b in range(ROWS // 4):
        word = jnp.broadcast_to(v[:, b // 8 : b // 8 + 1], (SEQS, 128))
        mask.append((lax.shift_right_logical(word, shift + (b % 8) * 4) & 1).astype(F32))
    out = total * jnp.concatenate(mask, axis=0)
    lbuf[slot, 0:16, :] = jnp.concatenate(masks, axis=0).astype(BF16)
    lbuf[slot, 16:L_ROWS, :] = out.astype(BF16)


def reorder_final(wv, wf, wt):
    wf[...] = wv[...].astype(F32)
    for n in range(8):
        rows = [wf[pl.ds(4 * n + e, WIDTH, stride=WIDTH), :] for e in range(4)]
        tile = jnp.concatenate(rows, axis=0).astype(BF16).T
        wt[n // 2, :, (n % 2) * 128 : (n % 2 + 1) * 128] = tile


def unpack_left(lbuf, part, a_ref, first):
    block = lbuf[:, 16 + L_STEP * part : 16 + L_STEP * (part + 1), :].astype(F32)
    groups = L_STEP // SEQS
    block = block.reshape(SLOTS, groups, SEQS, 128)
    for b in range(groups):
        tile = block[:, b].reshape(SLOTS * SEQS, 128).astype(BF16)
        a_ref[(first * groups + b) * 128 : (first * groups + b + 1) * 128, :] = tile.T


def unpack_right(rbuf, r_ref, part):
    block = rbuf[:, 16 + R_STEP * part : 16 + R_STEP * (part + 1), :].astype(F32)
    groups = R_STEP // SEQS
    block = block.reshape(SLOTS, groups, SEQS, COLS)
    for e in range(groups):
        r_ref[part, :, e * COLS : (e + 1) * COLS] = (
            block[:, e].reshape(SLOTS * SEQS, COLS).astype(BF16)
        )


def count_pairs(lbuf, rbuf, core, rc_ref):
    mi = lbuf[:, 0:16, :].astype(F32).reshape(SLOTS, 2, SEQS, 128)
    mj = rbuf[:, 0:16, :].astype(F32).reshape(SLOTS, 2, SEQS, 128)
    first = (core == 0).astype(F32)
    cols = (mj[:, 0] * first + mj[:, 1] * (1.0 - first)).reshape(128, 128).astype(BF16)
    for h in range(2):
        rows = mi[:, h].reshape(128, 128).astype(BF16)
        counts = lax.dot_general(rows, cols, (((0,), (0,)), ((), ())), preferred_element_type=F32)
        rc_ref[pl.ds(h * 128, 128), :] = 1.0 / jnp.maximum(counts, 1.0)


def outer_part(a, r, outer, block, first, count):
    for p in range(count // 2):
        x = jnp.dot(a, r[:, p * 256 : (p + 1) * 256], preferred_element_type=F32).astype(BF16)
        for i in range(block):
            for e in range(2):
                at = (first + 2 * p + e) * WIDTH
                outer[i // 2, at : at + WIDTH, (i % 2) * COLS : (i % 2 + 1) * COLS] = x[
                    i * WIDTH : (i + 1) * WIDTH, e * COLS : (e + 1) * COLS
                ]


def finish(y, rc, ob, k, put):
    for h in range(2):
        value = y[:, h * COLS : (h + 1) * COLS] * rc[2 * k + h : 2 * k + h + 1, :] + ob
        put(2 * k + h, value.astype(BF16).T)


def first_kernel(
    x_hbm, v_hbm, gain_hbm, ps_hbm, pt_hbm, w_hbm, off_hbm,
    out_hbm, a_ref, r_ref, wt_ref, rc_ref, ob_ref,
    xv, v_ref, gain_ref, ps_ref, pt_ref, wv, off_ref,
    wf, ns, nt, rs, rsend, lbuf, rbuf, near_a, outer, acc, stage,
    in_sem, out_sem, rs1, rr1, rs2, rr2, ls, lr, fs, fr,
):
    me = Place()
    loads = [
        pltpu.make_async_copy(src, dst, in_sem.at[n])
        for n, (src, dst) in enumerate([
            (x_hbm, xv), (v_hbm, v_ref), (gain_hbm, gain_ref), (pt_hbm, pt_ref), (ps_hbm, ps_ref),
            (off_hbm, off_ref), (w_hbm, wv),
        ])
    ]
    for load in loads:
        load.start()

    shifts = [(0, 1), (0, 2), (0, 3), (1, 0), (1, 1), (1, 2), (1, 3)]
    partner = me.device(core=1 - me.core)
    across = me.device(xh=1 - me.xh)
    beside = me.device(xl=1 - me.xl)
    along_z = [me.device(z=(me.z + b) % 4) for b in (1, 2, 3)]
    along_y = [me.device(y=(me.y + d) % 4) for d in (1, 2, 3)]
    froms = [((me.xh + a) % 2, (me.z + 4 - b) % 4) for a, b in shifts]
    relays = [me.device(y=me.relay_y, xl=me.relay_xl, xh=me.to_xh, z=me.to_z, core=h) for h in range(2)]
    sources = [
        me.device(y=me.from_y, xl=me.from_xl, xh=me.near_xh, z=me.near_z, core=c) for c in range(2)
    ]
    near = me.near_z * 4 + me.near_xh * 2
    bar = pltpu.get_barrier_semaphore()
    friends = [partner, across, beside] + along_z + along_y + relays + sources
    for device in friends:
        pl.semaphore_signal(bar, inc=1, device_id=device, device_id_type=MESH)

    def remote(src, dst, send, recv, device):
        return pltpu.make_async_remote_copy(
            src_ref=src, dst_ref=dst, send_sem=send, recv_sem=recv,
            device_id=device, device_id_type=MESH,
        )

    def first_copy(part, h):
        rows = span(R_STEP, part)
        return remote(
            rsend.at[h, rows], rbuf.at[me.slot, rows],
            rs1.at[part, h], rr1.at[part, me.core], relays[h],
        )

    def second_copy(part, n):
        pair = near if n < 4 else me.near_z * 4 + (1 - me.near_xh) * 2
        block = rbuf.at[pl.ds(pair, 2), span(R_STEP, part)]
        device = beside if n == 3 else along_y[n % 4]
        return remote(block, block, rs2.at[part, n], rr2.at[part, n], device)

    def left_copy(part, n):
        slot = me.slot if n < 4 or n == 7 else me.z * 4 + (1 - me.xh) * 2 + me.core
        piece = lbuf.at[slot, span(L_STEP, part)]
        device = partner if n == 7 else across if n == 3 else along_z[n % 4]
        return remote(piece, piece, ls.at[part, n], lr.at[part, n], device)

    def pass_on_copy(part, n):
        xh, z = froms[n]
        piece = lbuf.at[z * 4 + xh * 2 + me.core, span(L_STEP, part)]
        return remote(piece, piece, fs.at[part, n], fr.at[part, n], partner)

    def start_first(part):
        rows = span(R_STEP, part)
        for h, device in enumerate(relays):
            mine = me.is_me(device)

            @pl.when(jnp.logical_not(mine))
            def _():
                first_copy(part, h).start()

            @pl.when(mine)
            def _():
                rbuf[me.slot, rows, :] = rsend[h, rows, :]

    def relay(part):
        rows = span(R_STEP, part)
        for c, device in enumerate(sources):
            @pl.when(jnp.logical_not(me.is_me(device)))
            def _():
                remote(
                    rsend.at[0, rows], rbuf.at[near + c, rows], rs1.at[part, 0], rr1.at[part, c], device
                ).wait_recv()
        for n in (3, 0, 1, 2):
            second_copy(part, n).start()

    def relay_beside(part):
        second_copy(part, 3).wait_recv()
        for n in (4, 5, 6):
            second_copy(part, n).start()

    def start_left(part):
        for n in (3, 7, 0, 1, 2):
            left_copy(part, n).start()

    def relay_across(part):
        left_copy(part, 3).wait_recv()
        for n in (4, 5, 6):
            left_copy(part, n).start()
        pass_on_copy(part, 3).start()

    def pass_on(part):
        for n in (0, 1, 2, 4, 5, 6):
            left_copy(part, n).wait_recv()
            pass_on_copy(part, n).start()

    def take_right(part):
        for n in (0, 1, 2, 4, 5, 6):
            second_copy(part, n).wait_recv()
        unpack_right(rbuf, r_ref, part)

    def wait_left(part):
        left_copy(part, 7).wait_recv()
        for n in range(7):
            pass_on_copy(part, n).wait_recv()

    def step(part, block):
        rows = L_STEP // SEQS * 128
        outer_part(near_a[block * rows : (block + 1) * rows, :], r_ref.at[part], outer, STEP, 0, 8)
        for k in range(STEP // 2):
            y = jnp.dot(wt_ref[part], outer[k], preferred_element_type=F32)
            at = block * (STEP // 2) + k
            if part == 0:
                acc[at] = y
            elif part < PARTS - 1:
                acc[at] += y
            else:
                def put(i, value):
                    stage[block * STEP + i] = value

                rc = rc_ref[block * STEP : (block + 1) * STEP, :]
                finish(acc[at] + y, rc, ob_ref[...], k, put)

    def out_copy(block):
        rows = pl.ds(block * STEP, STEP)
        return pltpu.make_async_copy(stage.at[rows], out_hbm.at[rows], out_sem.at[block])

    for load in loads[:5]:
        load.wait()
    v = v_ref[...]
    masks = masks_by_half(v)
    normalise(xv, gain_ref, ns, nt)
    project_right(nt, pt_ref, masks, rs, rsend)
    pl.semaphore_wait(bar, len(friends))
    start_first(0)
    start_first(1)
    project_left(ns, ps_ref, v, masks, lbuf, me.slot)
    start_left(0)
    start_left(1)
    start_first(2)
    start_first(3)
    start_left(2)
    start_left(3)

    for load in loads[5:]:
        load.wait()
    reorder_final(wv, wf, wt_ref)
    ob_ref[...] = jnp.broadcast_to(off_ref[...], (CZ, CZ)).T

    relay(0)
    relay_across(0)
    relay(1)
    relay_beside(0)
    relay_across(1)
    relay(2)
    relay(3)
    relay_beside(1)
    pass_on(0)
    relay_across(2)
    take_right(0)
    wait_left(0)
    unpack_left(lbuf, 0, near_a, 0)
    step(0, 0)
    relay_beside(2)
    relay_across(3)
    relay_beside(3)
    pass_on(1)
    count_pairs(lbuf, rbuf, me.core, rc_ref)
    wait_left(1)
    unpack_left(lbuf, 1, near_a, 1)
    step(0, 1)
    take_right(1)
    step(1, 0)
    pass_on(2)
    step(1, 1)
    take_right(2)
    step(2, 0)
    pass_on(3)
    step(2, 1)
    take_right(3)
    step(3, 0)
    out_copy(0).start()
    for part in (2, 3):
        wait_left(part)
        unpack_left(lbuf, part, a_ref, part - 2)
    step(3, 1)
    out_copy(1).start()

    out_copy(0).wait()
    out_copy(1).wait()
    for part in range(PARTS):
        for h, device in enumerate(relays):
            @pl.when(jnp.logical_not(me.is_me(device)))
            def _():
                first_copy(part, h).wait_send()
        for n in range(7):
            second_copy(part, n).wait_send()
        for n in range(8):
            left_copy(part, n).wait_send()
        for n in range(7):
            pass_on_copy(part, n).wait_send()


def first_half(x, v, gain, ps, pt, w, off):
    vmem = pl.BlockSpec(memory_space=pltpu.VMEM)
    hbm = pl.BlockSpec(memory_space=pltpu.HBM)
    dma = pltpu.SemaphoreType.DMA
    return pl.pallas_call(
        first_kernel,
        out_shape=[
            jax.ShapeDtypeStruct((HALF, COLS, CZ), BF16),
            jax.ShapeDtypeStruct((HALF * WIDTH, 128), BF16),
            jax.ShapeDtypeStruct((PARTS, 128, WIDTH // PARTS * COLS), BF16),
            jax.ShapeDtypeStruct((PARTS, CZ, WIDTH // PARTS * WIDTH), BF16),
            jax.ShapeDtypeStruct((ROWS, COLS), F32),
            jax.ShapeDtypeStruct((CZ, CZ), F32),
        ],
        in_specs=[hbm] * 7,
        out_specs=[hbm] + [vmem] * 5,
        scratch_shapes=[
            pltpu.VMEM((SEQS, DEPTH, ROWS), BF16),
            pltpu.VMEM((SEQS, SEQS), jnp.int32),
            pltpu.VMEM((1, DEPTH), F32),
            pltpu.VMEM((WIDTH, DEPTH), BF16),
            pltpu.VMEM((WIDTH, DEPTH), BF16),
            pltpu.VMEM((WIDTH * WIDTH, CZ), BF16),
            pltpu.VMEM((1, CZ), F32),
            pltpu.VMEM((WIDTH * WIDTH, CZ), F32),
            pltpu.VMEM((SEQS * ROWS, DEPTH), F32),
            pltpu.VMEM((SEQS, DEPTH, ROWS), BF16),
            pltpu.VMEM((2, WIDTH * SEQS, COLS), F32),
            pltpu.VMEM((2, R_ROWS, COLS), BF16),
            pltpu.VMEM((SLOTS, L_ROWS, 128), BF16),
            pltpu.VMEM((SLOTS, R_ROWS, COLS), BF16),
            pltpu.VMEM((HALF * WIDTH, 128), BF16),
            pltpu.VMEM((STEP // 2, WIDTH // PARTS * WIDTH, 2 * COLS), BF16),
            pltpu.VMEM((HALF // 2, CZ, 2 * COLS), F32),
            pltpu.VMEM((HALF, COLS, CZ), BF16),
            dma((7,)), dma((2,)),
            dma((PARTS, 2)), dma((PARTS, 2)), dma((PARTS, 7)), dma((PARTS, 7)),
            dma((PARTS, 8)), dma((PARTS, 8)), dma((PARTS, 7)), dma((PARTS, 7)),
        ],
        compiler_params=pltpu.CompilerParams(
            collective_id=0, has_side_effects=True, vmem_limit_bytes=40 * 2**20
        ),
        name="gather_and_first_half",
    )(x, v, gain, ps, pt, w, off)


def second_kernel(half_hbm, a_ref, r_ref, wt_ref, rc_ref, ob_ref, out_hbm, outer, stage, sem):
    carry = pltpu.make_async_copy(half_hbm, out_hbm.at[pl.ds(0, HALF)], sem.at[2])
    carry.start()

    def out_copy(t, slot):
        return pltpu.make_async_copy(
            stage.at[slot], out_hbm.at[pl.ds(HALF + t * BLOCK, BLOCK)], sem.at[slot]
        )

    for t in range(HALF // BLOCK):
        slot = t % 2
        rows = BLOCK * WIDTH
        a = a_ref[t * rows : (t + 1) * rows, :]
        for part in range(PARTS):
            outer_part(a, r_ref.at[part], outer, BLOCK, part * 8, 8)
        if t >= 2:
            out_copy(t - 2, slot).wait()
        rc = rc_ref[HALF + t * BLOCK : HALF + (t + 1) * BLOCK, :]
        ob = ob_ref[...]
        w = jnp.concatenate([wt_ref[part] for part in range(PARTS)], axis=1)

        def put(i, value):
            stage[slot, i] = value

        for k in range(BLOCK // 2):
            y = jnp.dot(w, outer[k], preferred_element_type=F32)
            finish(y, rc, ob, k, put)
        out_copy(t, slot).start()
    out_copy(HALF // BLOCK - 2, 0).wait()
    out_copy(HALF // BLOCK - 1, 1).wait()
    carry.wait()


def second_half(half, a, r, wt, rc, ob):
    vmem = pl.BlockSpec(memory_space=pltpu.VMEM)
    hbm = pl.BlockSpec(memory_space=pltpu.HBM)
    return pl.pallas_call(
        second_kernel,
        in_specs=[hbm] + [vmem] * 5,
        out_specs=hbm,
        out_shape=jax.ShapeDtypeStruct((ROWS, COLS, CZ), BF16),
        scratch_shapes=[
            pltpu.VMEM((BLOCK // 2, WIDTH * WIDTH, 2 * COLS), BF16),
            pltpu.VMEM((2, BLOCK, COLS, CZ), BF16),
            pltpu.SemaphoreType.DMA((3,)),
        ],
        compiler_params=pltpu.CompilerParams(vmem_limit_bytes=32 * 2**20),
        name="second_half",
    )(half, a, r, wt, rc, ob)


def on_device(x, v, gain, ps, pt, w, off):
    inputs = (x.transpose(0, 2, 1), v, gain.reshape(1, DEPTH), ps.T, pt.T, w, off.reshape(1, CZ))
    return second_half(*first_half(*[pltpu.with_memory_space_constraint(a, pltpu.HBM) for a in inputs]))


def solution(mesh):
    in_specs = (P("col", "row", None), P("col", "row"), P(), P(), P(), P(), P())
    return jax.shard_map(
        on_device, mesh=mesh, in_specs=in_specs, out_specs=P("row", "col", None), check_vma=False
    )
```

time: 84.1 us -> 58.9 us (0.70)
  Pallas kernels: 74.2 us -> 58.6 us
  local copies, waits for them, and re-layouts: 9.56 us -> 0 us
    pallas_call x2, Pallas kernels: 74.2 us -> 58.6 us  [the longest x1 43.9 us: first_half(): pl.pallas_call(first_kernel, out_shape=[jax.ShapeDtypeStruct((HALF, COLS,...]
    unnamed x24 -> x0, local copies, waits for them, and re-layouts: 9.56 us -> none
where the time goes in v2:
time: 58.9 us; the launch traced here: 58.8 us
  Pallas kernels  58.6 us (99%)
    pallas_call x1, Pallas kernels, first_half(): pl.pallas_call(first_kernel, out_shape=[jax.ShapeDtypeStruct((HALF, COLS,...  43.9 us
    pallas_call x1, Pallas kernels, second_half(): pl.pallas_call(second_kernel, in_specs=[hbm] + [vmem] * 5, out_specs=hbm,...  14.8 us

profile of v2, /device:TPU:33, one launch (start us, length us, event | category | flops | bytes accessed | tf_op | source)
XLA Modules:
  0.0 58.8 jit_solution(6066141499601182689)
XLA Ops:
  0.0 43.9 %gather_and_first_half.1 = (bf16[128,128,128]{2,1,0:T(8,128)(2,1)S(1)}, bf16[4096,128]{1,0:T(8,128)(2,1)S(1)}, bf16[4,128,1024]{2,1,0:T(8,128)(2,1)S(1)}, bf16[4...) custom-call(bf16[8,64,256]{2,1,0:T(8,128)(2,1)} %bitcast.5, s32[8,8]{1,0:T(8,128)} %v_hbm.1, ...), custom_call_target="tpu_custom_call" | custom-call | tf_op jit(solution)/shard_map/gather_and_first_half/pallas_call | solution.py:390
  43.9 14.8 %second_half.1 = bf16[256,128,128]{2,1,0:T(8,128)(2,1)} custom-call(bf16[128,128,128]{2,1,0:T(8,128)(2,1)S(1)} %get-tuple-element.11.half_hbm, bf16[4096,128]{1,0:T(8,128)(2,1)S(1)} %get-tuple-element.12.a_ref, bf16[4,128,1024]{2,1,0:T(8,128)(2,1)S(1)} %get-tuple-element.13.r_ref, bf16[4,128,256]{2,1,0:T(8,128)(2,1)S(1)} %get-tuple-element.14.wt_ref, ...), custom_call_target="tpu_custom_call" | custom-call | tf_op jit(solution)/shard_map/second_half/pallas_call | solution.py:468

commit v3 on v2

--- a/solution.py
+++ b/solution.py
@@ -39,12 +39,17 @@
         self.xh, self.z, self.core = chip // 4, chip % 4, self.col % 2
         self.slot = self.z * 4 + self.xh * 2 + self.core
         self.to_xh, self.to_z = self.y // 2, self.row % 4
-        self.relay_y = (self.y + self.z - self.to_z + 4) % 4
+        turn, shift = self.turn(self.y, self.xl)
+        self.relay_y = (self.y + turn * (self.z - self.to_z + 4) + shift) % 4
         self.relay_xl = (self.xl + self.xh + self.to_xh) % 2
         self.from_y, self.from_xl = self.xh * 2 + self.z // 2, self.z % 2
 
-        self.near_z = (self.y - self.from_y + self.z + 4) % 4
+        turn, shift = self.turn(self.from_y, self.from_xl)
+        self.near_z = (self.z + turn * (self.y - self.from_y - shift + 8)) % 4
         self.near_xh = (self.xl + self.from_xl + self.xh) % 2
+
+    def turn(self, y, xl):
+        return 1 + 2 * (y % 2), xl * (3 - 2 * (y % 2))
 
     def device(self, y=None, xl=None, xh=None, z=None, core=None):
         pick = lambda a, b: b if a is None else a
@@ -169,10 +174,10 @@
 
 def first_kernel(
     x_hbm, v_hbm, gain_hbm, ps_hbm, pt_hbm, w_hbm, off_hbm,
-    out_hbm, a_ref, r_ref, wt_ref, rc_ref, ob_ref,
+    half_ref, a_ref, r_ref, wt_ref, rc_ref, ob_ref,
     xv, v_ref, gain_ref, ps_ref, pt_ref, wv, off_ref,
-    wf, ns, nt, rs, rsend, lbuf, rbuf, near_a, outer, acc, stage,
-    in_sem, out_sem, rs1, rr1, rs2, rr2, ls, lr, fs, fr,
+    wf, ns, nt, rs, rsend, lbuf, rbuf, near_a, outer, acc,
+    in_sem, rs1, rr1, rs2, rr2, ls, lr, fs, fr,
 ):
     me = Place()
     loads = [
@@ -262,7 +267,11 @@
             second_copy(part, n).start()
 
     def start_left(part):
-        for n in (3, 7, 0, 1, 2):
+        left_copy(part, 3).start()
+        left_copy(part, 7).start()
+
+    def left_z(part):
+        for n in range(3):
             left_copy(part, n).start()
 
     def relay_across(part):
@@ -298,14 +307,10 @@
                 acc[at] += y
             else:
                 def put(i, value):
-                    stage[block * STEP + i] = value
+                    half_ref[block * STEP + i] = value
 
                 rc = rc_ref[block * STEP : (block + 1) * STEP, :]
                 finish(acc[at] + y, rc, ob_ref[...], k, put)
-
-    def out_copy(block):
-        rows = pl.ds(block * STEP, STEP)
-        return pltpu.make_async_copy(stage.at[rows], out_hbm.at[rows], out_sem.at[block])
 
     for load in loads[:5]:
         load.wait()
@@ -317,12 +322,14 @@
     start_first(0)
     start_first(1)
     project_left(ns, ps_ref, v, masks, lbuf, me.slot)
-    start_left(0)
-    start_left(1)
+    for part in (0, 1):
+        start_left(part)
+        left_z(part)
     start_first(2)
     start_first(3)
-    start_left(2)
-    start_left(3)
+    for part in (2, 3):
+        start_left(part)
+        left_z(part)
 
     for load in loads[5:]:
         load.wait()
@@ -348,28 +355,25 @@
     relay_beside(3)
     pass_on(1)
     count_pairs(lbuf, rbuf, me.core, rc_ref)
+    take_right(1)
+    step(1, 0)
     wait_left(1)
     unpack_left(lbuf, 1, near_a, 1)
     step(0, 1)
-    take_right(1)
-    step(1, 0)
-    pass_on(2)
     step(1, 1)
     take_right(2)
+    pass_on(2)
     step(2, 0)
     pass_on(3)
     step(2, 1)
     take_right(3)
     step(3, 0)
-    out_copy(0).start()
-    for part in (2, 3):
-        wait_left(part)
-        unpack_left(lbuf, part, a_ref, part - 2)
+    wait_left(2)
+    unpack_left(lbuf, 2, a_ref, 0)
     step(3, 1)
-    out_copy(1).start()
-
-    out_copy(0).wait()
-    out_copy(1).wait()
+    wait_left(3)
+    unpack_left(lbuf, 3, a_ref, 1)
+
     for part in range(PARTS):
         for h, device in enumerate(relays):
             @pl.when(jnp.logical_not(me.is_me(device)))
@@ -398,7 +402,7 @@
             jax.ShapeDtypeStruct((CZ, CZ), F32),
         ],
         in_specs=[hbm] * 7,
-        out_specs=[hbm] + [vmem] * 5,
+        out_specs=[vmem] * 6,
         scratch_shapes=[
             pltpu.VMEM((SEQS, DEPTH, ROWS), BF16),
             pltpu.VMEM((SEQS, SEQS), jnp.int32),
@@ -417,8 +421,7 @@
             pltpu.VMEM((HALF * WIDTH, 128), BF16),
             pltpu.VMEM((STEP // 2, WIDTH // PARTS * WIDTH, 2 * COLS), BF16),
             pltpu.VMEM((HALF // 2, CZ, 2 * COLS), F32),
-            pltpu.VMEM((HALF, COLS, CZ), BF16),
-            dma((7,)), dma((2,)),
+            dma((7,)),
             dma((PARTS, 2)), dma((PARTS, 2)), dma((PARTS, 7)), dma((PARTS, 7)),
             dma((PARTS, 8)), dma((PARTS, 8)), dma((PARTS, 7)), dma((PARTS, 7)),
         ],
@@ -429,8 +432,8 @@
     )(x, v, gain, ps, pt, w, off)
 
 
-def second_kernel(half_hbm, a_ref, r_ref, wt_ref, rc_ref, ob_ref, out_hbm, outer, stage, sem):
-    carry = pltpu.make_async_copy(half_hbm, out_hbm.at[pl.ds(0, HALF)], sem.at[2])
+def second_kernel(half_ref, a_ref, r_ref, wt_ref, rc_ref, ob_ref, out_hbm, outer, stage, sem):
+    carry = pltpu.make_async_copy(half_ref, out_hbm.at[pl.ds(0, HALF)], sem.at[2])
     carry.start()
 
     def out_copy(t, slot):
@@ -467,7 +470,7 @@
     hbm = pl.BlockSpec(memory_space=pltpu.HBM)
     return pl.pallas_call(
         second_kernel,
-        in_specs=[hbm] + [vmem] * 5,
+        in_specs=[vmem] * 6,
         out_specs=hbm,
         out_shape=jax.ShapeDtypeStruct((ROWS, COLS, CZ), BF16),
         scratch_shapes=[

time: 58.9 us -> 58.4 us (level)
  Pallas kernels: 58.6 us -> 58 us
    pallas_call x1, Pallas kernels: 43.9 us -> 43 us  [first_half(): pl.pallas_call(first_kernel, out_shape=[jax.ShapeDtypeStruct((HALF, COLS,...]
where the time goes in v3:
time: 58.4 us; the launch traced here: 58.2 us
  Pallas kernels  58 us (99%)
    pallas_call x1, Pallas kernels, first_half(): pl.pallas_call(first_kernel, out_shape=[jax.ShapeDtypeStruct((HALF, COLS,...  43 us
    pallas_call x1, Pallas kernels, second_half(): pl.pallas_call(second_kernel, in_specs=[vmem] * 6, out_specs=hbm, out_sha...  15 us

profile of v3, /device:TPU:33, one launch (start us, length us, event | category | flops | bytes accessed | tf_op | source)
XLA Modules:
  0.0 58.2 jit_solution(4930763368148841645)
XLA Ops:
  0.0 43.0 %gather_and_first_half.1 = (bf16[128,128,128]{2,1,0:T(8,128)(2,1)S(1)}, bf16[4096,128]{1,0:T(8,128)(2,1)S(1)}, bf16[4,128,1024]{2,1,0:T(8,128)(2,1)S(1)}, bf16[4...) custom-call(bf16[8,64,256]{2,1,0:T(8,128)(2,1)} %bitcast.5, s32[8,8]{1,0:T(8,128)} %v_hbm.1, ...), custom_call_target="tpu_custom_call" | custom-call | tf_op jit(solution)/shard_map/gather_and_first_half/pallas_call | solution.py:394
  43.0 15.0 %second_half.1 = bf16[256,128,128]{2,1,0:T(8,128)(2,1)} custom-call(bf16[128,128,128]{2,1,0:T(8,128)(2,1)S(1)} %get-tuple-element.11.half_ref, bf16[4096,128]{1,0:T(8,128)(2,1)S(1)} %get-tuple-element.12.a_ref, bf16[4,128,1024]{2,1,0:T(8,128)(2,1)S(1)} %get-tuple-element.13.r_ref, bf16[4,128,256]{2,1,0:T(8,128)(2,1)S(1)} %get-tuple-element.14.wt_ref, ...), custom_call_target="tpu_custom_call" | custom-call | tf_op jit(solution)/shard_map/second_half/pallas_call | solution.py:471
